TPU v7x, 512 devices: a whole 4x8x8 slice. The times are simulated.
512 devices in a mesh: section: 4 (over x), seq: 128 (over z, y, core).
Axes of the slice: x: 4, y: 8, z: 8, core: 2. Of those that a mesh axis runs over, the one named last changes fastest.
Arguments:
- hidden: bfloat16 [65536, 4096], P('seq', 'section'), may hold values from -6 to 6
- norm_gain: bfloat16 [4096], P('section'), may hold values from 0.25 to 1.75
- query_weight: bfloat16 [4096, 512], P(None, 'section')
- key_weight: bfloat16 [4096, 128], P('section')
- value_weight: bfloat16 [4096, 128], P('section'), may hold values from -0.5 to 0.5
- output_weight: bfloat16 [512, 4096], P(None, 'section'), may hold values from -0.25 to 0.25
- block_reach: int32 [512], P('seq'), may hold values from 0 to 2
- header_ids: int32 [2], replicated, may hold values from 0 to 511, as said below
Outputs:
- attention_out: bfloat16 [65536, 4096], P('seq', 'section')
Inputs may be any that keep to these rules, and one draw needn't show every extreme that they name: `header_ids`: the 2 indices are distinct block indices, and the last block, 511, is always one of them, at any position.
All inputs are finite; a program needn't handle non-finite values.
Results may differ from a plain program's by a relative error of at most 0.014.
Values may be sent and summed in bfloat16 or wider, within the bound.
No kernel may reach another device: no remote copies, remote signals or barrier semaphores. Data moves between devices by JAX's collectives and lax.ppermute only.
A program may use at most 64 MiB of HBM per device.

v0:
```python
import math
import jax
import jax.numpy as jnp
from jax import lax
from jax.sharding import PartitionSpec as P

BLOCK = 128
REACH = 2
EPSILON = 1e-05
THETA = 500000.0


def merged(value, axis, combine):
    everything = jax.tree.map(lambda part: lax.all_gather(part, axis), value)
    leading = jax.tree.map(lambda part: part[0], everything)

    def lap(k, so_far):
        return combine(so_far, jax.tree.map(lambda part: part[k], everything))

    return lax.fori_loop(1, lax.axis_size(axis), lap, leading)


def padded(cells, sides, width):
    for axis, dim in sides:
        count = lax.axis_size(axis)
        ends = count - 1
        head = lax.slice_in_dim(cells, 0, width, axis=dim)
        tail = lax.slice_in_dim(cells, cells.shape[dim] - width, cells.shape[dim], axis=dim)
        cells = jnp.concatenate(
            [
                lax.ppermute(tail, axis, [(i, (i + 1) % count) for i in range(ends)]),
                cells,
                lax.ppermute(head, axis, [((i + 1) % count, i) for i in range(ends)]),
            ],
            axis=dim,
        )
    return cells


def tables(positions, head_width):
    middle = head_width // 2
    frequency = jnp.exp(
        -(2.0 / head_width) * math.log(THETA) * jnp.arange(middle, dtype=jnp.float32)
    )
    angles = positions.astype(jnp.float32)[:, None] * frequency[None, :]
    angles = jnp.concatenate([angles, angles], axis=1)
    return (jnp.cos(angles), jnp.sin(angles))


def rotate(values, cosine_table, sine_table):
    middle = values.shape[-1] // 2
    turned = jnp.concatenate([-values[..., middle:], values[..., :middle]], axis=-1)
    return values * cosine_table + turned * sine_table


def combine_parts(earlier, later):
    first_max, first_total, first_out = earlier
    second_max, second_total, second_out = later
    overall = jnp.maximum(first_max, second_max)
    first_factor = jnp.exp(first_max - overall)
    second_factor = jnp.exp(second_max - overall)
    return (
        overall,
        first_total * first_factor + second_total * second_factor,
        first_out * first_factor[:, None] + second_out * second_factor[:, None],
    )


def on_device(
    hidden,
    norm_gain,
    query_weight,
    key_weight,
    value_weight,
    output_weight,
    block_reach,
    header_ids,
):
    row_count = hidden.shape[0]
    part_width = hidden.shape[1]
    head_width = key_weight.shape[1]
    local_blocks = row_count // BLOCK
    total_blocks = local_blocks * lax.axis_size("seq")
    seq_place = lax.axis_index("seq")
    floats = hidden.astype(jnp.float32)
    squares = lax.psum(jnp.sum(floats * floats, axis=1), "section")
    scaling = lax.rsqrt(squares / (part_width * lax.axis_size("section")) + EPSILON)
    normed_part = (floats * scaling[:, None] * norm_gain.astype(jnp.float32)[None, :]).astype(
        jnp.bfloat16
    )
    weight_rows = query_weight
    query_sum = jnp.dot(
        lax.all_gather(normed_part, "section", axis=1, tiled=True),
        weight_rows,
        preferred_element_type=jnp.float32,
    )
    key_sum, value_sum = lax.psum(
        (
            jnp.dot(normed_part, key_weight, preferred_element_type=jnp.float32),
            jnp.dot(normed_part, value_weight, preferred_element_type=jnp.float32),
        ),
        "section",
    )
    positions = seq_place * row_count + jnp.arange(row_count, dtype=jnp.int32)
    cosine_table, sine_table = tables(positions, head_width)
    queries = rotate(query_sum, cosine_table, sine_table).astype(jnp.bfloat16)
    keys_here = rotate(key_sum, cosine_table, sine_table).astype(jnp.bfloat16)
    values_here = value_sum.astype(jnp.bfloat16)
    packed = jnp.concatenate([queries, keys_here, values_here], axis=1)
    block_numbers = seq_place * local_blocks + jnp.arange(local_blocks, dtype=jnp.int32)
    select = header_ids[:, None] == block_numbers[None, :]
    shaped = packed.reshape(local_blocks, BLOCK, 3 * head_width)
    picked = jnp.einsum(
        "hb,bre->hre", select.astype(jnp.bfloat16), shaped, preferred_element_type=jnp.float32
    )
    header_pack = lax.psum(picked, "seq").astype(jnp.bfloat16).reshape(-1, 3 * head_width)
    head_queries = header_pack[:, :head_width]
    head_keys = header_pack[:, head_width : 2 * head_width]
    head_values = header_pack[:, 2 * head_width :]
    inverse_root = 1.0 / math.sqrt(head_width)
    far_scores = (
        jnp.einsum("qd,kd->qk", head_queries, keys_here, preferred_element_type=jnp.float32)
        * inverse_root
    )
    far_max = jnp.max(far_scores, axis=1)
    far_weights = jnp.exp(far_scores - far_max[:, None])
    far_total = jnp.sum(far_weights, axis=1)
    far_out = jnp.dot(
        far_weights.astype(jnp.bfloat16), values_here, preferred_element_type=jnp.float32
    )
    merged_max, merged_total, merged_out = merged(
        (far_max, far_total, far_out), "seq", combine_parts
    )
    header_result = merged_out / merged_total[:, None]
    margin_rows = REACH * BLOCK
    stacked = jnp.concatenate([keys_here, values_here], axis=1)
    extended = padded(stacked, (("seq", 0),), margin_rows)
    near_keys = extended[:, :head_width]
    near_values = extended[:, head_width:]
    extent = row_count + 2 * margin_rows
    key_blocks = seq_place * local_blocks - REACH + jnp.arange(extent, dtype=jnp.int32) // BLOCK
    query_blocks = seq_place * local_blocks + jnp.arange(row_count, dtype=jnp.int32) // BLOCK
    limits = jnp.repeat(block_reach, BLOCK)
    key_header = jnp.any(header_ids[:, None] == key_blocks[None, :], axis=0)
    allowed = (key_blocks >= 0)[None, :] & (key_blocks < total_blocks)[None, :]
    allowed = allowed & (jnp.abs(key_blocks[None, :] - query_blocks[:, None]) <= limits[:, None])
    allowed = allowed & jnp.logical_not(key_header)[None, :]
    near_scores = (
        jnp.einsum("qd,kd->qk", queries, near_keys, preferred_element_type=jnp.float32)
        * inverse_root
    )
    near_scores = jnp.where(allowed, near_scores, -jnp.inf)
    head_scores = (
        jnp.einsum("qd,kd->qk", queries, head_keys, preferred_element_type=jnp.float32)
        * inverse_root
    )
    scores = jnp.concatenate([near_scores, head_scores], axis=1)
    row_top = jnp.max(scores, axis=1)
    weights = jnp.exp(scores - row_top[:, None])
    row_sums = jnp.sum(weights, axis=1)
    joined = jnp.concatenate([near_values, head_values], axis=0)
    mixed_out = (
        jnp.dot(weights.astype(jnp.bfloat16), joined, preferred_element_type=jnp.float32)
        / row_sums[:, None]
    )
    header_local = jnp.einsum(
        "hb,hre->bre", select.astype(jnp.float32), header_result.reshape(-1, BLOCK, head_width)
    )
    is_local_header = jnp.any(select, axis=0)
    attended = jnp.where(
        is_local_header[:, None, None],
        header_local,
        mixed_out.reshape(local_blocks, BLOCK, head_width),
    )
    attended = attended.reshape(row_count, head_width).astype(jnp.bfloat16)
    weight_rows = output_weight
    result = jnp.dot(
        lax.all_gather(attended, "section", axis=1, tiled=True),
        weight_rows,
        preferred_element_type=jnp.float32,
    )
    return result.astype(jnp.bfloat16)


def solution(mesh):
    return jax.shard_map(
        on_device,
        mesh=mesh,
        in_specs=(
            P("seq", "section"),
            P("section"),
            P(None, "section"),
            P("section", None),
            P("section", None),
            P(None, "section"),
            P("seq"),
            P(),
        ),
        out_specs=P("seq", "section"),
        check_vma=False,
    )
```

profile of v0, /device:TPU:64, one launch (start us, length us, event | category | flops | bytes accessed | tf_op | source)
XLA Modules:
  0.0 913.6 jit_solution(16988144689448362159)
XLA Ops:
  7.3 1.5 fusion.2
  8.8 10.5 %psum.28 = f32[512]{0:T(512)S(1)} all-reduce(f32[512]{0:T(512)S(1)} %fusion.2), channel_id=1, replica_groups=mesh['section'=4,'seq'=128] {'section'}, use_global_device_ids=true, to_apply=%region_2.0 | all-reduce | flops 512 | bytes 4096 | tf_op jit(solution)/shard_map/psum | solution.py:86
  19.3 1.6 fusion.4
  20.9 1.2 fusion.53
  23.0 1.7 fusion.54
  24.8 17.2 %all-reduce.5 = bf16[512,128]{0,1:T(8,128)(2,1)S(1)} all-reduce(f32[512,128]{0,1:T(8,128)S(1)} %fusion.54), channel_id=1, replica_groups=mesh['section'=4,'seq'=128] {'section'}, use_global_device_ids=true, to_apply=%region_4.0 | all-reduce | flops 65536 | bytes 393216 | tf_op jit(solution)/shard_map/psum | solution.py:97
  42.0 34.5 %all-reduce.4.cloned.1.call-done = f32[512,128]{0,1:T(8,128)} async-done(((f32[512,128]{0,1:T(8,128)}), f32[512,128]{0,1:T(8,128)}) %all-reduce.4.cloned.1.call-update) | async-done | bytes 262160 | tf_op jit(solution)/shard_map/psum | solution.py:97
  77.5 55.5 %all-gather.8.cloned.1.call-done = bf16[512,4096]{1,0:T(8,128)(2,1)} async-done(((bf16[512,1024]{1,0:T(8,128)(2,1)}), bf16[512,4096]{1,0:T(8,128)(2,1)}) %all-gather.8.cloned.1.call-update) | async-done | bytes 4194320 | tf_op jit(solution)/shard_map/all_gather | solution.py:93
  133.0 3.7 fusion.52
  138.7 461.0 %all-reduce.6 = bf16[2,128,384]{2,0,1:T(2,128)(2,1)S(1)} all-reduce(f32[2,128,384]{2,0,1:T(2,128)S(1)} %fusion.48), channel_id=1, replica_groups=mesh['section'=4,'seq'=128] {'seq'}, use_global_device_ids=true, to_apply=%region_5.0 | all-reduce | flops 98304 | bytes 589824 | tf_op jit(solution)/shard_map/psum | solution.py:116
  601.6 82.4 %all-gather.3 = f32[128,1,256]{2,1,0:T(1,128)S(1)} all-gather(f32[1,1,256]{2,1,0:T(1,128)S(1)} %bitcast.66), channel_id=2, replica_groups=mesh['section'=4,'seq'=128] {'seq'}, dimensions={0}, use_global_device_ids=true | all-gather | bytes 132096 | tf_op jit(solution)/shard_map/all_gather | solution.py:14
  684.3 47.1 %all-gather.4 = f32[128,1,256]{2,1,0:T(1,128)S(1)} all-gather(f32[1,1,256]{2,1,0:T(1,128)S(1)} %bitcast.67), channel_id=3, replica_groups=mesh['section'=4,'seq'=128] {'seq'}, dimensions={0}, use_global_device_ids=true | all-gather | bytes 132096 | tf_op jit(solution)/shard_map/all_gather | solution.py:14
  731.4 4.6 collective-permute-start.1
  736.0 1.9 collective-permute-start
  738.5 5.9 collective-permute-done
  748.1 144.2 %while.19 = (s32[]{:T(128)}, f32[256]{0:T(256)S(1)}, f32[256]{0:T(256)S(1)}, f32[256,128]{1,0:T(8,128)S(1)}, f32[128,256]{1,0:T(8,128)S(1)}, /*index=5*/f32[128,...) while((s32[]{:T(128)}, f32[256]{0:T(256)S(1)}, f32[256]{0:T(256)S(1)}, ...), condition=%wide.region_9.10_spmd, body=%wide.region_8.0_spmd.sunk | while | flops 99845 | bytes 407703 | solution.py:20
  749.3 1.1 fusion.69
  751.5 1.1 fusion.69
  753.8 1.1 fusion.69
  754.9 1.1 fusion.69
  756.1 1.1 fusion.69
  757.2 1.1 fusion.69
  758.3 1.1 fusion.69
  759.5 1.1 fusion.69
  761.7 1.1 fusion.69
  764.0 1.1 fusion.69
  766.3 1.1 fusion.69
  768.6 1.1 fusion.69
  770.8 1.1 fusion.69
  773.1 1.1 fusion.69
  775.4 1.1 fusion.69
  776.5 1.1 fusion.69
  777.6 1.1 fusion.69
  778.8 1.1 fusion.69
  779.9 1.1 fusion.69
  781.1 1.1 fusion.69
  783.3 1.1 fusion.69
  785.6 1.1 fusion.69
  787.9 1.1 fusion.69
  790.1 1.1 fusion.69
  792.4 1.1 fusion.69
  794.7 1.1 fusion.69
  797.0 1.1 fusion.69
  798.1 1.1 fusion.69
  799.2 1.1 fusion.69
  800.4 1.1 fusion.69
  892.8 12.6 %all_gather.31 = bf16[512,512]{1,0:T(8,128)(2,1)S(1)} all-gather(bf16[512,128]{1,0:T(8,128)(2,1)S(1)} %bitcast.59), channel_id=1, replica_groups=mesh['section'=4,'seq'=128] {'section'}, dimensions={1}, use_global_device_ids=true | all-gather | bytes 655360 | tf_op jit(solution)/shard_map/all_gather | solution.py:178
  905.4 1.7 convolution_convert_fusion
  (426 shorter events, 119.3 us)
Async XLA Ops:
  6.5 898.9 %copy-start = (bf16[512,1024]{1,0:T(8,128)(2,1)S(1)}, bf16[512,1024]{1,0:T(8,128)(2,1)}, u32[]{:S(2)}) copy-start(bf16[512,1024]{1,0:T(8,128)(2,1)} %param.15) | copy-start | bytes 3145732
  6.5 14.4 %copy-start.7 = (bf16[1024,128]{1,0:T(8,128)(2,1)S(1)}, bf16[1024,128]{1,0:T(8,128)(2,1)}, u32[]{:S(2)}) copy-start(bf16[1024,128]{1,0:T(8,128)(2,1)} %param.13) | copy-start | bytes 786436
  6.5 70.0 %all-reduce.4.cloned.1.call-start = ((), (), s32[]{:S(2)}) async-start(), calls=%async_computation.1 | async-start | bytes 524288 | tf_op jit(solution)/shard_map/psum | solution.py:97
  19.3 3.6 copy-start.8
  20.9 1.3 copy-start.1
  22.1 110.9 %copy-start.4 = (bf16[4096,128]{1,0:T(8,128)(2,1)S(1)}, bf16[4096,128]{1,0:T(8,128)(2,1)}, u32[]{:S(2)}) copy-start(bf16[4096,128]{1,0:T(8,128)(2,1)} %param.12) | copy-start | bytes 3145732
  22.2 110.8 %all-gather.8.cloned.1.call-start = ((), (), s32[]{:S(2)}) async-start(), calls=%async_computation | async-start | bytes 5242880 | tf_op jit(solution)/shard_map/all_gather | solution.py:93
  22.9 724.2 %all-gather.10.cloned.1.call-start = ((), (), s32[]{:S(2)}) async-start(), calls=%async_computation.2 | async-start | bytes 16908288 | tf_op jit(solution)/shard_map/all_gather | solution.py:14
  77.5 59.2 %copy-start.3 = (f32[512,128]{0,1:T(8,128)S(1)}, f32[512,128]{0,1:T(8,128)}, u32[]{:S(2)}) copy-start(f32[512,128]{0,1:T(8,128)} %all-reduce.4.cloned.1.call-done) | copy-start | bytes 786436
  136.7 1.6 copy-start.9
  138.3 463.3 %copy-start.10 = (s32[4]{0:T(128)S(1)}, s32[4]{0:T(128)}, u32[]{:S(2)}) copy-start(s32[4]{0:T(128)} %param.16) | copy-start | bytes 52
  684.1 61.5 %copy-start.6 = (f32[128,1,256]{2,1,0:T(1,128)}, f32[128,1,256]{2,1,0:T(1,128)S(1)}, u32[]{:S(2)}) copy-start(f32[128,1,256]{2,1,0:T(1,128)S(1)} %all-gather.3) | copy-start | bytes 393220
  731.4 14.1 %copy-start.5 = (f32[128,1,256]{2,1,0:T(1,128)}, f32[128,1,256]{2,1,0:T(1,128)S(1)}, u32[]{:S(2)}) copy-start(f32[128,1,256]{2,1,0:T(1,128)S(1)} %all-gather.4) | copy-start | bytes 393220
  731.4 7.1 collective-permute-start.1
  736.0 8.4 collective-permute-start
  744.5 1.1 copy-start.2
  745.6 1.0 slice-start
  746.5 1.5 slice-start.1
  746.5 1.5 slice-start.2
Sparse Core Ops, SparseCore 0:
  22.3 54.2 all-reduce.3
  78.9 54.1 all-gather.7
  601.4 126.7 all-gather.9
where the time goes:
time: 916 us; the launch traced here: 914 us
  blocking collectives  631 us (69%)
  other arithmetic  146 us (16%)
  waiting for transfers between devices  96.8 us (11%)
  between operations  13.5 us (1%)
  matrix products  12.3 us (1%)
    psum x1, blocking collectives, on_device(): lax.psum(picked, 'seq').astype(jnp.bfloat16).reshape(-1, 3 * head_width)  461 us
    add x127, other arithmetic, combine_parts(): first_out * first_factor[:, None] + second_out * second_factor[:, None]  136 us
    all_gather x2, blocking collectives, merged(): everything = jax.tree.map(lambda part: lax.all_gather(part, axis), value)  130 us
    all_gather x1, waiting for transfers between devices, on_device(): lax.all_gather(normed_part, 'section', axis=1, tiled=True)  55.5 us
    psum x1, waiting for transfers between devices, on_device(): lax.psum((jnp.dot(normed_part, key_weight, preferred_element_type=jnp.flo...  34.5 us
  transfers between devices with their start and end apart: 5, of which 4 were waited for; matrix products, arithmetic and copies ran while one was open for 1% of the time, Pallas kernels for 0%

commit v1 on v0

--- a/solution.py
+++ b/solution.py
@@ -3,11 +3,16 @@
 import jax.numpy as jnp
 from jax import lax
 from jax.sharding import PartitionSpec as P
+from jax.lax import all_gather
 
 BLOCK = 128
 REACH = 2
 EPSILON = 1e-05
 THETA = 500000.0
+
+
+def leaves_obtain(frame):
+    return all_gather(frame, "seq").sum(axis=0)
 
 
 def merged(value, axis, combine):
@@ -113,7 +118,7 @@
     picked = jnp.einsum(
         "hb,bre->hre", select.astype(jnp.bfloat16), shaped, preferred_element_type=jnp.float32
     )
-    header_pack = lax.psum(picked, "seq").astype(jnp.bfloat16).reshape(-1, 3 * head_width)
+    header_pack = leaves_obtain(picked).astype(jnp.bfloat16).reshape(-1, 3 * head_width)
     head_queries = header_pack[:, :head_width]
     head_keys = header_pack[:, head_width : 2 * head_width]
     head_values = header_pack[:, 2 * head_width :]

time: 916 us -> 625 us (0.68)
  blocking collectives: 631 us -> 142 us
  waiting for transfers between devices: 96.8 us -> 275 us
  other arithmetic: 146 us -> 163 us
    psum x1 -> x0, blocking collectives: 461 us -> none  [on_device(): lax.psum(picked, 'seq').astype(jnp.bfloat16).reshape(-1, 3 * head_width)]
    all_gather x0 -> x1, waiting for transfers between devices: none -> 182 us  [leaves_obtain(): return all_gather(frame, 'seq').sum(axis=0)]
    all_gather x2, blocking collectives: 130 us -> 100 us  [merged(): everything = jax.tree.map(lambda part: lax.all_gather(part, axis), value)]
    reduce_sum x0 -> x1, other arithmetic: none -> 17.6 us  [leaves_obtain(): return all_gather(frame, 'seq').sum(axis=0)]
  transfers between devices with their start and end apart: 5 -> 6, of which waited for: 4 -> 5; matrix products, arithmetic and copies ran while one was open for 1% -> 1% of each run, Pallas kernels for 0% -> 0%
where the time goes in v1:
time: 625 us; the launch traced here: 622 us
  waiting for transfers between devices  275 us (44%)
  other arithmetic  163 us (26%)
  blocking collectives  142 us (23%)
  between operations  13.5 us (2%)
  matrix products  12.3 us (2%)
  starting transfers between devices  8.09 us (1%)
    all_gather x1, waiting for transfers between devices, leaves_obtain(): return all_gather(frame, 'seq').sum(axis=0)  182 us
    add x127, other arithmetic, combine_parts(): first_out * first_factor[:, None] + second_out * second_factor[:, None]  136 us
    all_gather x2, blocking collectives, merged(): everything = jax.tree.map(lambda part: lax.all_gather(part, axis), value)  100 us
    all_gather x1, waiting for transfers between devices, on_device(): lax.all_gather(normed_part, 'section', axis=1, tiled=True)  55.5 us
    psum x1, waiting for transfers between devices, on_device(): lax.psum((jnp.dot(normed_part, key_weight, preferred_element_type=jnp.flo...  34.5 us
    reduce_sum x1, other arithmetic, leaves_obtain(): return all_gather(frame, 'seq').sum(axis=0)  17.6 us
    psum x1, blocking collectives, on_device(): lax.psum((jnp.dot(normed_part, key_weight, preferred_element_type=jnp.flo...  17.2 us
    all_gather x1, blocking collectives, on_device(): lax.all_gather(attended, 'section', axis=1, tiled=True)  14.5 us
  transfers between devices with their start and end apart: 6, of which 5 were waited for; matrix products, arithmetic and copies ran while one was open for 1% of the time, Pallas kernels for 0%

profile of v1, /device:TPU:64, one launch (start us, length us, event | category | flops | bytes accessed | tf_op | source)
XLA Modules:
  0.0 622.4 jit_solution(1750948196864686670)
XLA Ops:
  6.5 1.6 fusion.2
  8.1 10.5 %psum.21 = f32[512]{0:T(512)S(1)} all-reduce(f32[512]{0:T(512)S(1)} %fusion.2), channel_id=1, replica_groups=mesh['section'=4,'seq'=128] {'section'}, use_global_device_ids=true, to_apply=%region_2.0 | all-reduce | flops 512 | bytes 4096 | tf_op jit(solution)/shard_map/psum | solution.py:91
  19.3 1.6 fusion.4
  20.9 1.2 fusion.53
  23.0 1.7 fusion.54
  24.8 17.2 %all-reduce.4 = bf16[512,128]{0,1:T(8,128)(2,1)S(1)} all-reduce(f32[512,128]{0,1:T(8,128)S(1)} %fusion.54), channel_id=1, replica_groups=mesh['section'=4,'seq'=128] {'section'}, use_global_device_ids=true, to_apply=%region_4.0 | all-reduce | flops 65536 | bytes 393216 | tf_op jit(solution)/shard_map/psum | solution.py:102
  42.0 34.5 %all-reduce.3.cloned.1.call-done = f32[512,128]{0,1:T(8,128)} async-done(((f32[512,128]{0,1:T(8,128)}), f32[512,128]{0,1:T(8,128)}) %all-reduce.3.cloned.1.call-update) | async-done | bytes 262160 | tf_op jit(solution)/shard_map/psum | solution.py:102
  77.5 55.5 %all-gather.10.cloned.1.call-done = bf16[512,4096]{1,0:T(8,128)(2,1)} async-done(((bf16[512,1024]{1,0:T(8,128)(2,1)}), bf16[512,4096]{1,0:T(8,128)(2,1)}) %all-gather.10.cloned.1.call-update) | async-done | bytes 4194320 | tf_op jit(solution)/shard_map/all_gather | solution.py:98
  133.0 3.7 fusion.52
  139.5 181.7 %all-gather.12.cloned.1.call-done = f32[256,128,384]{2,1,0:T(8,128)} async-done(((f32[2,128,384]{2,1,0:T(8,128)}), f32[256,128,384]{2,1,0:T(8,128)}) %all-gather.12.cloned.1.call-update) | async-done | bytes 50331664 | tf_op jit(solution)/shard_map/all_gather | solution.py:15
  321.2 17.6 %reduce_sum.37 = bf16[2,128,384]{2,1,0:T(8,128)(2,1)S(1)} reduce(f32[128,2,128,384]{3,2,1,0:T(8,128)} %bitcast.54, f32[]{:T(128)} %constant.86.clone.1), dimensions={0}, to_apply=%region_5.0 | reduce | flops 12484608 | bytes 50528260 | tf_op jit(solution)/shard_map/reduce_sum | solution.py:15
  340.5 2.2 collective-permute-start
  342.7 5.8 collective-permute-start.1
  349.2 1.8 collective-permute-done.1
  352.4 50.4 %all-gather.5 = f32[128,1,256]{2,1,0:T(1,128)S(1)} all-gather(f32[1,1,256]{2,1,0:T(1,128)S(1)} %bitcast.69), channel_id=4, replica_groups=mesh['section'=4,'seq'=128] {'seq'}, dimensions={0}, use_global_device_ids=true | all-gather | bytes 132096 | tf_op jit(solution)/shard_map/all_gather | solution.py:19
  402.9 49.6 %all-gather.4 = f32[128,1,256]{2,1,0:T(1,128)S(1)} all-gather(f32[1,1,256]{2,1,0:T(1,128)S(1)} %bitcast.68), channel_id=3, replica_groups=mesh['section'=4,'seq'=128] {'seq'}, dimensions={0}, use_global_device_ids=true | all-gather | bytes 132096 | tf_op jit(solution)/shard_map/all_gather | solution.py:19
  455.0 144.2 %while.19 = (s32[]{:T(128)}, f32[256]{0:T(256)S(1)}, f32[256]{0:T(256)S(1)}, f32[256,128]{1,0:T(8,128)S(1)}, f32[128,256]{1,0:T(8,128)S(1)}, /*index=5*/f32[128,...) while((s32[]{:T(128)}, f32[256]{0:T(256)S(1)}, f32[256]{0:T(256)S(1)}, ...), condition=%wide.region_9.10_spmd, body=%wide.region_8.0_spmd.sunk | while | flops 99845 | bytes 407703 | solution.py:25
  455.0 1.1 fusion.69
  457.3 1.1 fusion.69
  458.4 1.1 fusion.69
  459.6 1.1 fusion.69
  460.7 1.1 fusion.69
  461.8 1.1 fusion.69
  463.0 1.1 fusion.69
  465.2 1.1 fusion.69
  467.5 1.1 fusion.69
  469.8 1.1 fusion.69
  472.1 1.1 fusion.69
  474.3 1.1 fusion.69
  476.6 1.1 fusion.69
  478.9 1.1 fusion.69
  480.0 1.1 fusion.69
  481.1 1.1 fusion.69
  482.3 1.1 fusion.69
  483.4 1.1 fusion.69
  484.6 1.1 fusion.69
  486.8 1.1 fusion.69
  489.1 1.1 fusion.69
  491.4 1.1 fusion.69
  493.6 1.1 fusion.69
  495.9 1.1 fusion.69
  498.2 1.1 fusion.69
  500.5 1.1 fusion.69
  501.6 1.1 fusion.69
  502.7 1.1 fusion.69
  503.9 1.1 fusion.69
  599.7 14.5 %all_gather.39 = bf16[512,512]{1,0:T(8,128)(2,1)S(1)} all-gather(bf16[512,128]{1,0:T(8,128)(2,1)S(1)} %bitcast.59), channel_id=1, replica_groups=mesh['section'=4,'seq'=128] {'section'}, dimensions={1}, use_global_device_ids=true | all-gather | bytes 655360 | tf_op jit(solution)/shard_map/all_gather | solution.py:183
  614.2 1.7 convolution_convert_fusion
  (424 shorter events, 121.0 us)
Async XLA Ops:
  6.5 607.6 %copy-start = (bf16[512,1024]{1,0:T(8,128)(2,1)S(1)}, bf16[512,1024]{1,0:T(8,128)(2,1)}, u32[]{:S(2)}) copy-start(bf16[512,1024]{1,0:T(8,128)(2,1)} %param.15) | copy-start | bytes 3145732
  6.5 14.4 %copy-start.5 = (bf16[1024,128]{1,0:T(8,128)(2,1)S(1)}, bf16[1024,128]{1,0:T(8,128)(2,1)}, u32[]{:S(2)}) copy-start(bf16[1024,128]{1,0:T(8,128)(2,1)} %param.13) | copy-start | bytes 786436
  6.5 70.0 %all-reduce.3.cloned.1.call-start = ((), (), s32[]{:S(2)}) async-start(), calls=%async_computation.1 | async-start | bytes 524288 | tf_op jit(solution)/shard_map/psum | solution.py:102
  19.3 3.6 copy-start.6
  20.9 1.3 copy-start.1
  22.1 110.9 %copy-start.4 = (bf16[4096,128]{1,0:T(8,128)(2,1)S(1)}, bf16[4096,128]{1,0:T(8,128)(2,1)}, u32[]{:S(2)}) copy-start(bf16[4096,128]{1,0:T(8,128)(2,1)} %param.12) | copy-start | bytes 3145732
  22.1 110.8 %all-gather.10.cloned.1.call-start = ((), (), s32[]{:S(2)}) async-start(), calls=%async_computation | async-start | bytes 5242880 | tf_op jit(solution)/shard_map/all_gather | solution.py:98
  22.9 298.3 %all-gather.12.cloned.1.call-start = ((), (), s32[]{:S(2)}) async-start(), calls=%async_computation.2 | async-start | bytes 50724864 | tf_op jit(solution)/shard_map/all_gather | solution.py:15
  77.5 59.2 %copy-start.3 = (f32[512,128]{0,1:T(8,128)S(1)}, f32[512,128]{0,1:T(8,128)}, u32[]{:S(2)}) copy-start(f32[512,128]{0,1:T(8,128)} %all-reduce.3.cloned.1.call-done) | copy-start | bytes 786436
  136.7 1.6 copy-start.7
  139.5 314.6 %all-gather.14.cloned.1.call-start = ((), (), s32[]{:S(2)}) async-start(), calls=%async_computation.3 | async-start | bytes 16908288 | tf_op jit(solution)/shard_map/all_gather | solution.py:19
  338.8 1.6 copy-start.8
  340.5 8.7 %collective-permute-start = (bf16[256,256]{0,1:T(8,128)(2,1)S(1)}, bf16[256,256]{0,1:T(8,128)(2,1)S(1)}, u32[]{:S(2)}, u32[]{:S(2)}) collective-permute-start(bf16[256,256]{0,1:T(8,128)(2,1)S(1)} %get-tuple-element.204), channel_id=1, source_target_pairs={{0,1},{1,2},{2,3},{3,4},{4,5},{5,6},{6,7},{7,8},{8,9},{9,10},{10,1... | collective-permute-start | bytes 393224 | tf_op jit(solution)/shard_map/ppermute | solution.py:36
  342.7 8.3 %collective-permute-start.1 = (bf16[256,256]{0,1:T(8,128)(2,1)S(1)}, bf16[256,256]{0,1:T(8,128)(2,1)S(1)}, u32[]{:S(2)}, u32[]{:S(2)}) collective-permute-start(bf16[256,256]{0,1:T(8,128)(2,1)S(1)} %get-tuple-element.205), channel_id=1, source_target_pairs={{1,0},{2,1},{3,2},{4,3},{5,4},{6,5},{7,6},{8,7},{9,8},{10,9},{11,1... | collective-permute-start | bytes 393224 | tf_op jit(solution)/shard_map/ppermute | solution.py:38
  351.1 1.1 copy-start.2
  402.8 50.6 %slice-start = ((bf16[1024,256]{0,1:T(8,128)(2,1)}), bf16[1024,128]{0,1:T(8,128)(2,1)S(1)}, s32[]{:S(2)}) async-start(bf16[1024,256]{0,1:T(8,128)(2,1)} %copy-done.2), calls=%async_computation.4 | async-start | bytes 524288 | tf_op jit(solution)/shard_map/slice | solution.py:144
Sparse Core Ops, SparseCore 0:
  22.3 54.2 all-reduce.2
  78.8 54.1 all-gather.9
  139.6 181.5 all-gather.11
  340.4 98.8 all-gather.13
